TPU v7x, 128 devices: a whole 4x4x4 slice. The times are simulated.
128 devices in a mesh: team: 8 (over y_lo, z), rep: 16 (over x, y_hi, core).
Axes of the slice: x: 4, y: 4 (y_hi: 2, y_lo: 2; y = y_hi * 2 + y_lo), z: 4, core: 2. Of those that a mesh axis runs over, the one named last changes fastest.
Arguments:
- affinity: bfloat16 [8, 256, 8, 128, 128], P('team', 'rep'), as said below
- col_index: int32 [8, 256, 8], P('team', 'rep'), may hold values from 0 to 31, all different within a row
- labels: int32 [32768], P(('rep', 'team')), may hold values from 0 to 511
Outputs:
- diffused: bfloat16 [32768, 512], P(('rep', 'team'))
Inputs may be any that keep to these rules, and one draw needn't show every extreme that they name: `affinity`: every entry is positive. `col_index`: the 8 block columns of one block row are different.
All inputs are finite; a program needn't handle non-finite values.
Results may differ from a plain program's by a relative error of at most 0.017.
Values may be sent and summed in bfloat16 or wider, within the bound.
A program may use at most 128 MiB of HBM per device.

v0:
```python
import jax
import jax.numpy as jnp
from jax import lax
from jax.sharding import PartitionSpec as P

C = 512
ITERS = 3


def on_device(affinity, col_index, labels):
    panels = affinity[0]
    columns = col_index[0]
    block = panels.shape[-1]
    slots = panels.shape[1]
    rows_here = labels.shape[0]
    classes = jnp.arange(C, dtype=jnp.int32)
    seeded = (labels[:, None] == classes[None, :]).astype(jnp.float32) * 16.0
    current = seeded.astype(jnp.bfloat16)
    for step_index in range(ITERS):
        gathered = lax.all_gather(current, "rep", axis=0, tiled=True).reshape(-1, block, C)
        block_count = lax.axis_size("team") * rows_here // block
        summed = jnp.zeros((block_count, block, C), jnp.float32)
        for slot_index in range(slots):
            picked = gathered[columns[:, slot_index]]
            summed = summed + jnp.einsum(
                "iab,ibc->iac", panels[:, slot_index], picked, preferred_element_type=jnp.float32
            )
        summed_all = lax.psum_scatter(
            summed.reshape(lax.axis_size("team") * rows_here, C).astype(jnp.bfloat16),
            "team",
            scatter_dimension=0,
            tiled=True,
        ).astype(jnp.float32)
        blended = 0.9 * summed_all + 0.1 * seeded
        scale_rows = lax.rsqrt(jnp.mean(blended * blended, axis=-1, keepdims=True) + 1e-06)
        current = (blended * scale_rows).astype(jnp.bfloat16)
    return current


def solution(mesh):
    in_specs = (P("team", "rep", None, None, None), P("team", "rep", None), P(("rep", "team")))
    out_specs = P(("rep", "team"), None)
    return jax.shard_map(
        on_device, mesh=mesh, in_specs=in_specs, out_specs=out_specs, check_vma=False
    )
```

profile of v0, /device:TPU:0, one launch (start us, length us, event | category | flops | bytes accessed | tf_op | source)
XLA Modules:
  0.0 504.4 jit_solution(15811978290454994971)
XLA Ops:
  6.5 1.5 select_convert_fusion
  8.1 4.7 copy.6
  12.9 55.3 %all-gather.4.cloned.1.call-done = bf16[4096,512]{1,0:T(8,128)(2,1)} async-done(((bf16[256,512]{1,0:T(8,128)(2,1)}), bf16[4096,512]{1,0:T(8,128)(2,1)}) %all-gather.4.cloned.1.call-update) | async-done | bytes 4194320 | tf_op jit(solution)/shard_map/all_gather | solution.py:20
  68.2 2.9 gather_fusion.7
  71.1 4.2 gather_fusion.6
  75.3 4.2 gather_fusion.5
  79.5 4.2 gather_fusion.4
  83.7 4.3 gather_fusion.3
  87.9 4.2 gather_fusion.2
  92.1 4.2 gather_fusion.1
  96.3 4.2 gather_fusion
  100.5 2.6 fusion.21
  104.2 0.7 fusion.18
  104.9 0.9 copy-done.13
  105.8 2.7 fusion.15
  108.5 2.7 fusion.12
  111.2 2.6 fusion.9
  113.8 2.6 fusion.6
  116.5 2.7 fusion.3
  119.2 10.8 %add_convert_fusion.2 = bf16[16,512,128]{1,2,0:T(8,128)(2,1)} fusion(f32[16,512,128]{1,2,0:T(8,128)S(1)} %fusion.21, f32[16,512,128]{1,2,0:T(8,128)S(1)} %fusion.18, f32[16,512,128]{1,2,0:T(8,128)} %fusion.15, f32[16,512,128]{1,2,0:T(8,128)} %fusion.12, f32[16,512,128]{1,2,0:T(8,128)} %fusion.9, f32[16,512,128]{1,2,0:T(8,128)} %fusion.3, ...), kind=kOutput, calls=%fused_computation.27 | convolution fusion | flops 276824064 | bytes 34078720 | tf_op jit(solution)/shard_map/iab,ibc->iac/dot_general | solution.py:25
  130.1 41.6 %reduce-scatter.4.cloned.1.call-done = bf16[256,512]{1,0:T(8,128)(2,1)} async-done(((bf16[2048,512]{1,0:T(8,128)(2,1)}), bf16[256,512]{1,0:T(8,128)(2,1)}) %reduce-scatter.4.cloned.1.call-update) | async-done | bytes 262160 | tf_op jit(solution)/shard_map/reduce_scatter | solution.py:28
  171.7 1.2 multiply_reduce_fusion.2
  173.0 1.9 multiply_convert_fusion.2
  175.1 54.6 %all-gather.6.cloned.1.call-done = bf16[4096,512]{1,0:T(8,128)(2,1)} async-done(((bf16[256,512]{1,0:T(8,128)(2,1)}), bf16[4096,512]{1,0:T(8,128)(2,1)}) %all-gather.6.cloned.1.call-update) | async-done | bytes 4194320 | tf_op jit(solution)/shard_map/all_gather | solution.py:20
  229.7 2.9 gather_fusion.15
  232.6 4.2 gather_fusion.14
  236.8 4.3 gather_fusion.13
  241.0 4.2 gather_fusion.12
  245.2 4.2 gather_fusion.11
  249.4 4.2 gather_fusion.10
  253.6 4.2 gather_fusion.9
  257.8 4.2 gather_fusion.8
  262.0 2.6 fusion.22
  265.7 0.7 fusion.19
  266.3 0.9 copy-done.18
  267.2 2.7 fusion.16
  270.0 2.7 fusion.13
  272.7 2.6 fusion.10
  275.3 2.6 fusion.4
  277.9 2.7 fusion.7
  280.7 10.8 %add_convert_fusion.1 = bf16[16,512,128]{1,2,0:T(8,128)(2,1)} fusion(f32[16,512,128]{1,2,0:T(8,128)S(1)} %fusion.22, f32[16,512,128]{1,2,0:T(8,128)S(1)} %fusion.19, f32[16,512,128]{1,2,0:T(8,128)} %fusion.16, f32[16,512,128]{1,2,0:T(8,128)} %fusion.13, f32[16,512,128]{1,2,0:T(8,128)} %fusion.10, f32[16,512,128]{1,2,0:T(8,128)} %fusion.4, ...), kind=kOutput, calls=%fused_computation.26 | convolution fusion | flops 276824064 | bytes 34078720 | tf_op jit(solution)/shard_map/iab,ibc->iac/dot_general | solution.py:25
  291.6 41.8 %reduce-scatter.6.cloned.1.call-done = bf16[256,512]{1,0:T(8,128)(2,1)} async-done(((bf16[2048,512]{1,0:T(8,128)(2,1)}), bf16[256,512]{1,0:T(8,128)(2,1)}) %reduce-scatter.6.cloned.1.call-update) | async-done | bytes 262160 | tf_op jit(solution)/shard_map/reduce_scatter | solution.py:28
  333.4 1.2 multiply_reduce_fusion.1
  334.6 1.9 multiply_convert_fusion.1
  336.7 54.3 %all-gather.8.cloned.1.call-done = bf16[4096,512]{1,0:T(8,128)(2,1)} async-done(((bf16[256,512]{1,0:T(8,128)(2,1)}), bf16[4096,512]{1,0:T(8,128)(2,1)}) %all-gather.8.cloned.1.call-update) | async-done | bytes 4194320 | tf_op jit(solution)/shard_map/all_gather | solution.py:20
  391.1 2.9 gather_fusion.23
  393.9 4.2 gather_fusion.22
  398.1 4.2 gather_fusion.21
  402.3 4.2 gather_fusion.20
  406.5 4.3 gather_fusion.19
  410.7 4.2 gather_fusion.18
  415.0 4.2 gather_fusion.17
  419.1 4.2 gather_fusion.16
  423.4 2.6 fusion.5
  427.7 0.9 copy-done.17
  428.6 2.6 fusion.11
  431.2 2.7 fusion.14
  434.0 2.7 fusion.17
  436.7 2.6 fusion.20
  439.3 2.6 fusion.23
  441.9 10.7 %add_convert_fusion = bf16[16,512,128]{1,2,0:T(8,128)(2,1)} fusion(f32[16,512,128]{1,2,0:T(8,128)} %fusion.23, f32[16,512,128]{1,2,0:T(8,128)} %fusion.20, f32[16,512,128]{1,2,0:T(8,128)} %fusion.17, f32[16,512,128]{1,2,0:T(8,128)} %fusion.14, f32[16,512,128]{1,2,0:T(8,128)} %fusion.11, f32[16,512,128]{1,2,0:T(8,128)S(1)} %fusion.5, ...), kind=kOutput, calls=%fused_computation.25 | convolution fusion | flops 276824064 | bytes 34078720 | tf_op jit(solution)/shard_map/iab,ibc->iac/dot_general | solution.py:25
  452.6 41.8 %reduce-scatter.8.cloned.1.call-done = bf16[256,512]{1,0:T(8,128)(2,1)} async-done(((bf16[2048,512]{1,0:T(8,128)(2,1)}), bf16[256,512]{1,0:T(8,128)(2,1)}) %reduce-scatter.8.cloned.1.call-update) | async-done | bytes 262160 | tf_op jit(solution)/shard_map/reduce_scatter | solution.py:28
  494.5 1.2 multiply_reduce_fusion
  495.7 1.9 multiply_convert_fusion
  (64 shorter events, 4.7 us)
Async XLA Ops:
  6.5 61.7 %all-gather.4.cloned.1.call-start = ((), (), s32[]{:S(2)}) async-start(), calls=%async_computation.3 | async-start | bytes 4456448 | tf_op jit(solution)/shard_map/all_gather | solution.py:20
  8.1 4.8 copy-start.22
  8.1 163.6 %reduce-scatter.4.cloned.1.call-start = ((), (), s32[]{:S(2)}) async-start(), calls=%async_computation.4 | async-start | bytes 2359296 | tf_op jit(solution)/shard_map/reduce_scatter | solution.py:28
  100.5 3.0 copy-start
  100.5 3.7 copy-start.12
  104.2 1.6 copy-start.13
  105.8 2.7 copy-start.10
  108.5 2.7 copy-start.11
  111.2 2.6 copy-start.8
  113.8 2.6 copy-start.9
  130.0 41.7 %copy-start.21 = (s32[256]{0:T(256)S(1)}, s32[256]{0:T(256)}, u32[]{:S(2)}) copy-start(s32[256]{0:T(256)} %param.5) | copy-start | bytes 3076
  130.0 99.7 %all-gather.6.cloned.1.call-start = ((), (), s32[]{:S(2)}) async-start(), calls=%async_computation.5 | async-start | bytes 4456448 | tf_op jit(solution)/shard_map/all_gather | solution.py:20
  174.8 158.5 %reduce-scatter.6.cloned.1.call-start = ((), (), s32[]{:S(2)}) async-start(), calls=%async_computation.6 | async-start | bytes 2359296 | tf_op jit(solution)/shard_map/reduce_scatter | solution.py:28
  262.0 3.0 copy-start.1
  262.0 3.7 copy-start.19
  265.7 1.6 copy-start.18
  267.2 2.7 copy-start.16
  270.0 2.7 copy-start.14
  272.7 2.6 copy-start.15
  275.3 2.6 copy-start.6
  291.5 99.5 %all-gather.8.cloned.1.call-start = ((), (), s32[]{:S(2)}) async-start(), calls=%async_computation.7 | async-start | bytes 4456448 | tf_op jit(solution)/shard_map/all_gather | solution.py:20
  336.5 158.0 %reduce-scatter.8.cloned.1.call-start = ((), (), s32[]{:S(2)}) async-start(), calls=%async_computation.8 | async-start | bytes 2359296 | tf_op jit(solution)/shard_map/reduce_scatter | solution.py:28
  423.3 3.0 copy-start.2
  423.4 3.7 copy-start.20
  427.0 1.6 copy-start.17
  428.6 2.6 copy-start.7
  431.2 2.7 copy-start.5
  434.0 2.7 copy-start.4
  436.7 2.6 copy-start.3
Sparse Core Ops, SparseCore 0:
  9.8 58.4 all-gather.3
  130.2 41.5 reduce-scatter.3
  175.0 54.6 all-gather.5
  291.6 41.6 reduce-scatter.5
  336.6 54.4 all-gather.7
  452.8 41.6 reduce-scatter.7
where the time goes:
time: 506 us; the launch traced here: 504 us
  waiting for transfers between devices  290 us (57%)
  local copies, waits for them, and re-layouts  108 us (21%)
  matrix products  82.3 us (16%)
  between operations  13.6 us (3%)
  other arithmetic  10.8 us (2%)
    all_gather x3, waiting for transfers between devices, on_device(): lax.all_gather(current, 'rep', axis=0, tiled=True).reshape(-1, block, C)  164 us
    reduce_scatter x3, waiting for transfers between devices, on_device(): lax.psum_scatter(summed.reshape(lax.axis_size('team') * rows_here, C).ast...  125 us
    gather x24, local copies, waits for them, and re-layouts, on_device(): picked = gathered[columns[:, slot_index]]  96.9 us
    dot_general x24, matrix products, on_device(): jnp.einsum('iab,ibc->iac', panels[:, slot_index], picked, preferred_eleme...  82.3 us
    unnamed x47, local copies, waits for them, and re-layouts  10.7 us
  transfers between devices with their start and end apart: 6, of which 6 were waited for; matrix products, arithmetic and copies ran while one was open for 1% of the time, Pallas kernels for 0%

commit v1 on v0

--- a/solution.py
+++ b/solution.py
@@ -5,6 +5,12 @@
 
 C = 512
 ITERS = 3
+
+
+def close_patch(field_in, peer_axis):
+    return jnp.concatenate(
+        lax.all_to_all(jnp.stack(lax.axis_size(peer_axis) * [field_in], 0), peer_axis, 0, 0), axis=0
+    )
 
 
 def on_device(affinity, col_index, labels):
@@ -17,7 +23,7 @@
     seeded = (labels[:, None] == classes[None, :]).astype(jnp.float32) * 16.0
     current = seeded.astype(jnp.bfloat16)
     for step_index in range(ITERS):
-        gathered = lax.all_gather(current, "rep", axis=0, tiled=True).reshape(-1, block, C)
+        gathered = close_patch(current, "rep").reshape(-1, block, C)
         block_count = lax.axis_size("team") * rows_here // block
         summed = jnp.zeros((block_count, block, C), jnp.float32)
         for slot_index in range(slots):

time: 506 us -> 514 us (1.016)
  blocking collectives: 0 us -> 116 us
  waiting for transfers between devices: 290 us -> 174 us
  starting transfers between devices: 0.61 us -> 7.29 us
    all_gather x3 -> x0, waiting for transfers between devices: 164 us -> none  [on_device(): lax.all_gather(current, 'rep', axis=0, tiled=True).reshape(-1, block, C)]
    all_to_all x0 -> x2, blocking collectives: none -> 116 us  [close_patch(): lax.all_to_all(jnp.stack(lax.axis_size(peer_axis) * [field_in], 0), peer_...]
    all_to_all x0 -> x1, waiting for transfers between devices: none -> 47.6 us  [close_patch(): lax.all_to_all(jnp.stack(lax.axis_size(peer_axis) * [field_in], 0), peer_...]
    all_to_all x0 -> x1, starting transfers between devices: none -> 7.17 us  [close_patch(): lax.all_to_all(jnp.stack(lax.axis_size(peer_axis) * [field_in], 0), peer_...]
  transfers between devices with their start and end apart: 6 -> 4, of which waited for: 6 -> 4; matrix products, arithmetic and copies ran while one was open for 1% -> 1% of each run, Pallas kernels for 0% -> 0%
where the time goes in v1:
time: 514 us; the launch traced here: 512 us
  waiting for transfers between devices  174 us (34%)
  blocking collectives  116 us (23%)
  local copies, waits for them, and re-layouts  111 us (22%)
  matrix products  82 us (16%)
  between operations  13.3 us (3%)
  other arithmetic  8.66 us (2%)
  starting transfers between devices  7.29 us (1%)
    reduce_scatter x3, waiting for transfers between devices, on_device(): lax.psum_scatter(summed.reshape(lax.axis_size('team') * rows_here, C).ast...  127 us
    all_to_all x2, blocking collectives, close_patch(): lax.all_to_all(jnp.stack(lax.axis_size(peer_axis) * [field_in], 0), peer_...  116 us
    gather x24, local copies, waits for them, and re-layouts, on_device(): picked = gathered[columns[:, slot_index]]  96.9 us
    dot_general x24, matrix products, on_device(): jnp.einsum('iab,ibc->iac', panels[:, slot_index], picked, preferred_eleme...  82 us
    all_to_all x1, waiting for transfers between devices, close_patch(): lax.all_to_all(jnp.stack(lax.axis_size(peer_axis) * [field_in], 0), peer_...  47.6 us
    unnamed x47, local copies, waits for them, and re-layouts  10.7 us
  transfers between devices with their start and end apart: 4, of which 4 were waited for; matrix products, arithmetic and copies ran while one was open for 1% of the time, Pallas kernels for 0%

profile of v1, /device:TPU:0, one launch (start us, length us, event | category | flops | bytes accessed | tf_op | source)
XLA Modules:
  0.0 512.4 jit_solution(9077920641586104583)
XLA Ops:
  6.5 0.8 select_convert_fusion
  7.3 2.4 stack.6
  9.7 7.2 %all-to-all-start = ((bf16[16,256,512]{2,1,0:T(8,128)(2,1)}), bf16[16,256,512]{2,1,0:T(8,128)(2,1)}, u32[]{:S(2)}, u32[]{:S(2)}) async-start(bf16[16,256,512]{2,1,0:T(8,128)(2,1)} %stack.6), calls=%async_computation | async-start | bytes 8388608 | tf_op jit(solution)/shard_map/all_to_all | solution.py:12
  16.9 4.7 copy.6
  21.7 47.6 %all-to-all-done = bf16[16,256,512]{2,1,0:T(8,128)(2,1)} async-done(((bf16[16,256,512]{2,1,0:T(8,128)(2,1)}), bf16[16,256,512]{2,1,0:T(8,128)(2,1)}, u32[]{:S(2)}, u32[]{:S(2)}) %all-to-all-start) | async-done | bytes 4194336 | tf_op jit(solution)/shard_map/all_to_all | solution.py:12
  69.3 2.9 gather_fusion.7
  72.2 4.2 gather_fusion.6
  76.4 4.2 gather_fusion.5
  80.6 4.2 gather_fusion.4
  84.8 4.3 gather_fusion.3
  89.0 4.2 gather_fusion.2
  93.2 4.2 gather_fusion.1
  97.4 4.2 gather_fusion
  101.6 2.6 fusion.21
  106.0 0.9 copy-done.13
  106.9 2.7 fusion.15
  109.6 2.7 fusion.12
  112.2 2.6 fusion.9
  114.9 2.6 fusion.6
  117.5 2.7 fusion.3
  120.2 10.8 %add_convert_fusion.2 = bf16[16,512,128]{1,2,0:T(8,128)(2,1)} fusion(f32[16,512,128]{1,2,0:T(8,128)S(1)} %fusion.21, f32[16,512,128]{1,2,0:T(8,128)S(1)} %fusion.18, f32[16,512,128]{1,2,0:T(8,128)} %fusion.15, f32[16,512,128]{1,2,0:T(8,128)} %fusion.12, f32[16,512,128]{1,2,0:T(8,128)} %fusion.9, f32[16,512,128]{1,2,0:T(8,128)} %fusion.3, ...), kind=kOutput, calls=%fused_computation.27 | convolution fusion | flops 276824064 | bytes 34078720 | tf_op jit(solution)/shard_map/iab,ibc->iac/dot_general | solution.py:31
  131.1 51.4 %reduce-scatter.4.cloned.1.call-done = bf16[256,512]{1,0:T(8,128)(2,1)} async-done(((bf16[2048,512]{1,0:T(8,128)(2,1)}), bf16[256,512]{1,0:T(8,128)(2,1)}) %reduce-scatter.4.cloned.1.call-update) | async-done | bytes 262160 | tf_op jit(solution)/shard_map/reduce_scatter | solution.py:34
  182.5 1.2 multiply_reduce_fusion.2
  183.7 1.1 multiply_convert_fusion.2
  185.3 58.2 %all_to_all.15 = bf16[16,256,512]{2,1,0:T(8,128)(2,1)} all-to-all(bf16[16,256,512]{2,1,0:T(8,128)(2,1)S(1)} %stack.7), channel_id=1, replica_groups=mesh['team'=8,'rep'=16] {'rep'}, dimensions={0} | all-to-all | bytes 8388608 | tf_op jit(solution)/shard_map/all_to_all | solution.py:12
  243.5 2.9 gather_fusion.15
  246.4 4.2 gather_fusion.14
  250.5 4.3 gather_fusion.13
  254.8 4.2 gather_fusion.12
  259.0 4.2 gather_fusion.11
  263.2 4.2 gather_fusion.10
  267.4 4.2 gather_fusion.9
  271.6 4.2 gather_fusion.8
  275.8 2.6 fusion.22
  280.1 0.9 copy-done.18
  281.0 2.7 fusion.16
  283.7 2.7 fusion.13
  286.4 2.6 fusion.10
  289.0 2.6 fusion.4
  291.7 2.7 fusion.7
  294.4 10.8 %add_convert_fusion.1 = bf16[16,512,128]{1,2,0:T(8,128)(2,1)} fusion(f32[16,512,128]{1,2,0:T(8,128)S(1)} %fusion.22, f32[16,512,128]{1,2,0:T(8,128)S(1)} %fusion.19, f32[16,512,128]{1,2,0:T(8,128)} %fusion.16, f32[16,512,128]{1,2,0:T(8,128)} %fusion.13, f32[16,512,128]{1,2,0:T(8,128)} %fusion.10, f32[16,512,128]{1,2,0:T(8,128)} %fusion.4, ...), kind=kOutput, calls=%fused_computation.26 | convolution fusion | flops 276824064 | bytes 34078720 | tf_op jit(solution)/shard_map/iab,ibc->iac/dot_general | solution.py:31
  305.2 37.5 %reduce-scatter.6.cloned.1.call-done = bf16[256,512]{1,0:T(8,128)(2,1)} async-done(((bf16[2048,512]{1,0:T(8,128)(2,1)}), bf16[256,512]{1,0:T(8,128)(2,1)}) %reduce-scatter.6.cloned.1.call-update) | async-done | bytes 262160 | tf_op jit(solution)/shard_map/reduce_scatter | solution.py:34
  342.7 1.2 multiply_reduce_fusion.1
  344.0 1.1 multiply_convert_fusion.1
  345.5 58.0 %all_to_all.16 = bf16[16,256,512]{2,1,0:T(8,128)(2,1)} all-to-all(bf16[16,256,512]{2,1,0:T(8,128)(2,1)S(1)} %stack.8), channel_id=1, replica_groups=mesh['team'=8,'rep'=16] {'rep'}, dimensions={0} | all-to-all | bytes 8388608 | tf_op jit(solution)/shard_map/all_to_all | solution.py:12
  403.6 2.9 gather_fusion.23
  406.5 4.2 gather_fusion.22
  410.7 4.2 gather_fusion.21
  414.9 4.2 gather_fusion.20
  419.1 4.3 gather_fusion.19
  423.3 4.2 gather_fusion.18
  427.5 4.2 gather_fusion.17
  431.7 4.2 gather_fusion.16
  435.9 2.6 fusion.5
  440.3 0.9 copy-done.17
  441.2 2.6 fusion.11
  443.8 2.7 fusion.14
  446.5 2.7 fusion.17
  449.2 2.6 fusion.20
  451.8 2.6 fusion.23
  454.4 10.7 %add_convert_fusion = bf16[16,512,128]{1,2,0:T(8,128)(2,1)} fusion(f32[16,512,128]{1,2,0:T(8,128)} %fusion.23, f32[16,512,128]{1,2,0:T(8,128)} %fusion.20, f32[16,512,128]{1,2,0:T(8,128)} %fusion.17, f32[16,512,128]{1,2,0:T(8,128)} %fusion.14, f32[16,512,128]{1,2,0:T(8,128)} %fusion.11, f32[16,512,128]{1,2,0:T(8,128)S(1)} %fusion.5, ...), kind=kOutput, calls=%fused_computation.25 | convolution fusion | flops 276824064 | bytes 34078720 | tf_op jit(solution)/shard_map/iab,ibc->iac/dot_general | solution.py:31
  465.1 37.7 %reduce-scatter.8.cloned.1.call-done = bf16[256,512]{1,0:T(8,128)(2,1)} async-done(((bf16[2048,512]{1,0:T(8,128)(2,1)}), bf16[256,512]{1,0:T(8,128)(2,1)}) %reduce-scatter.8.cloned.1.call-update) | async-done | bytes 262160 | tf_op jit(solution)/shard_map/reduce_scatter | solution.py:34
  502.8 1.2 multiply_reduce_fusion
  504.1 1.9 multiply_convert_fusion
  (62 shorter events, 6.3 us)
Async XLA Ops:
  9.7 59.6 %all-to-all-start = ((bf16[16,256,512]{2,1,0:T(8,128)(2,1)}), bf16[16,256,512]{2,1,0:T(8,128)(2,1)}, u32[]{:S(2)}, u32[]{:S(2)}) async-start(bf16[16,256,512]{2,1,0:T(8,128)(2,1)} %stack.6), calls=%async_computation | async-start | bytes 8388608 | tf_op jit(solution)/shard_map/all_to_all | solution.py:12
  16.9 4.8 copy-start.22
  16.9 165.6 %reduce-scatter.4.cloned.1.call-start = ((), (), s32[]{:S(2)}) async-start(), calls=%async_computation.6 | async-start | bytes 2359296 | tf_op jit(solution)/shard_map/reduce_scatter | solution.py:34
  101.6 3.0 copy-start
  101.6 3.7 copy-start.12
  105.3 1.6 copy-start.13
  106.9 2.7 copy-start.10
  109.6 2.7 copy-start.11
  112.2 2.6 copy-start.8
  114.9 2.6 copy-start.9
  131.0 51.5 %copy-start.21 = (s32[256]{0:T(256)S(1)}, s32[256]{0:T(256)}, u32[]{:S(2)}) copy-start(s32[256]{0:T(256)} %param.5) | copy-start | bytes 3076
  131.0 211.7 %reduce-scatter.6.cloned.1.call-start = ((), (), s32[]{:S(2)}) async-start(), calls=%async_computation.7 | async-start | bytes 2359296 | tf_op jit(solution)/shard_map/reduce_scatter | solution.py:34
  275.8 3.0 copy-start.1
  275.8 3.7 copy-start.19
  279.4 1.6 copy-start.18
  281.0 2.7 copy-start.16
  283.7 2.7 copy-start.14
  286.4 2.6 copy-start.15
  289.0 2.6 copy-start.6
  305.2 197.6 %reduce-scatter.8.cloned.1.call-start = ((), (), s32[]{:S(2)}) async-start(), calls=%async_computation.8 | async-start | bytes 2359296 | tf_op jit(solution)/shard_map/reduce_scatter | solution.py:34
  435.9 3.0 copy-start.2
  435.9 3.7 copy-start.20
  439.6 1.6 copy-start.17
  441.2 2.6 copy-start.7
  443.8 2.7 copy-start.5
  446.5 2.7 copy-start.4
  449.2 2.6 copy-start.3
Sparse Core Ops, SparseCore 0:
  131.1 51.2 reduce-scatter.3
  305.3 37.3 reduce-scatter.5
  465.2 37.5 reduce-scatter.7
